TPU v7x, 512 devices: a whole 4x4x16 slice. The times are simulated.
512 devices in a mesh: row: 64 (over y, z_lo, core), pair: 8 (over z_hi, x).
Axes of the slice: x: 4, y: 4, z: 16 (z_hi: 2, z_lo: 8; z = z_hi * 8 + z_lo), core: 2. Of those that a mesh axis runs over, the one named last changes fastest.
Arguments:
- matrix: float32 [32768, 8192], P('row', 'pair'), may hold values from -100 to 100
- rotations: float32 [2, 8, 1024, 1024], P(None, 'pair', 'row'), may hold values from -0.1875 to 0.1875
Outputs:
- rotated: float32 [32768, 8192], P('row', 'pair')
- coupling: float32 [2, 8, 512, 512], P(None, 'pair', 'row')
All inputs are finite; a program needn't handle non-finite values.
Results may differ from a plain program's by a relative error of at most 0.00012.
Values sent between devices are 32-bit elements; how exact they have to be, the bound alone decides.
A program may use at most 64 MiB of HBM per device.

v0:
```python
import jax
import jax.numpy as jnp
from jax import lax
from jax.sharding import PartitionSpec as P

HIGH = lax.Precision.HIGHEST


def passed_along(value, axis, steps):
    count = lax.axis_size(axis)
    first, last = (max(0, -steps), min(count, count - steps))
    return lax.ppermute(value, axis, [(source, source + steps) for source in range(first, last)])


def couple(top, bottom):
    block = top.shape[1]
    total = top.shape[0] * lax.axis_size("row")
    share = block // lax.axis_size("row")
    first = lax.axis_index("row") * share
    cross = lax.dot_general(
        top, bottom, (((0,), (0,)), ((), ())), precision=HIGH, preferred_element_type=jnp.float32
    )
    cross, norm_top, norm_bottom = lax.psum(
        (cross, jnp.sum(top * top, axis=0), jnp.sum(bottom * bottom, axis=0)), "row"
    )
    cross = lax.dynamic_slice_in_dim(cross, first, share, 0)
    mean_top = lax.dynamic_slice_in_dim(norm_top, first, share, 0) / total + 1e-06
    mean_bottom = norm_bottom / total + 1e-06
    scale = jnp.sqrt(jnp.float32(total)) * jnp.sqrt(mean_top[:, None] * mean_bottom[None, :])
    return cross / scale


def per_device(matrix, rotations):
    block = matrix.shape[1] // 2
    rounds = rotations.shape[0]
    where_pair = lax.axis_index("pair")
    last_pair = lax.axis_size("pair") - 1
    top = matrix[:, :block]
    bottom = matrix[:, block:]
    couplings = []
    for step in range(rounds):
        couplings.append(couple(top, bottom))
        joined = jnp.concatenate([top, bottom], axis=1)
        transform = lax.all_gather(rotations[step, 0], "row", axis=0, tiled=True)
        turned = jnp.dot(joined, transform, precision=HIGH, preferred_element_type=jnp.float32)
        top = turned[:, :block]
        bottom = turned[:, block:]
        if step + 1 < rounds:
            outgoing = jnp.where(where_pair == 0, bottom, top)
            arrived_top = passed_along(outgoing, "pair", 1)
            arrived_bottom = passed_along(bottom, "pair", -1)
            next_top = jnp.where(where_pair == 0, top, arrived_top)
            bottom = jnp.where(where_pair == last_pair, top, arrived_bottom)
            top = next_top
    rotated = jnp.concatenate([top, bottom], axis=1)
    return (rotated, jnp.stack(couplings)[:, None])


def solution(mesh):
    in_specs = (P("row", "pair"), P(None, "pair", "row", None))
    out_specs = (P("row", "pair"), P(None, "pair", "row", None))
    return jax.shard_map(
        per_device, mesh=mesh, in_specs=in_specs, out_specs=out_specs, check_vma=False
    )
```

profile of v0, /device:TPU:1, one launch (start us, length us, event | category | flops | bytes accessed | tf_op | source)
XLA Modules:
  0.0 1162.7 jit_solution(18415072599138998580)
XLA Ops:
  7.2 0.0 all-gather.5.cloned.1.call-start
  7.2 1.5 fusion.11
  8.7 0.0 all-gather.5.cloned.1.call-update
  8.8 0.0 all-gather.7.cloned.1.call-start
  8.8 0.7 all-gather.7.cloned.1.call-update
  9.5 0.0 all-reduce.4.cloned.1.call-start
  9.6 129.8 %all-gather.5.cloned.1.call-done = f32[1,1,1024,1024]{3,2,1,0:T(8,128)} async-done(((f32[1,1,16,1024]{3,2,1,0:T(8,128)}), f32[1,1,1024,1024]{3,2,1,0:T(8,128)}) %all-gather.5.cloned.1.call-update) | async-done | bytes 4194320 | tf_op jit(solution)/shard_map/all_gather | solution.py:44
  139.3 9.6 fusion.2
  149.0 0.0 copy-start.1
  149.0 0.0 copy-start
  149.0 1.6 slice_select_fusion.2
  150.6 0.5 copy-done.1
  151.1 3.2 collective-permute-start
  154.3 1.3 collective-permute-start.1
  155.6 0.0 copy-done
  155.6 0.0 copy-start.2
  155.7 2.8 fusion.7
  158.5 18.4 %collective-permute-done = f32[512,512]{1,0:T(8,128)S(1)} collective-permute-done((f32[512,512]{1,0:T(8,128)}, f32[512,512]{1,0:T(8,128)S(1)}, u32[]{:S(2)}, u32[]{:S(2)}) %collective-permute-start) | collective-permute-done | bytes 1048608 | tf_op jit(solution)/shard_map/ppermute | solution.py:12
  176.9 0.0 copy-start.4
  176.9 1.0 copy-done.4
  177.9 2.8 collective-permute-done.1
  180.7 0.0 copy-done.2
  180.7 1.6 multiply_reduce_fusion.1
  182.4 0.0 copy-start.3
  182.4 1.0 copy-done.3
  183.4 2.9 fusion.12
  186.3 0.0 all-reduce.4.cloned.1.call-update
  186.3 0.2 multiply_reduce_fusion.3
  186.5 245.7 %all-reduce = (f32[512]{0:T(512)S(1)}, f32[512]{0:T(512)S(1)}, f32[512]{0:T(512)S(1)}, f32[512]{0:T(512)S(1)}) all-reduce(f32[512]{0:T(512)S(1)} %get-tuple-element.16, f32[512]{0:T(512)S(1)} %get-tuple-element.12, f32[512]{0:T(512)S(1)} %get-tuple-element.5, f32[512]{0:T(512)S(1)} %get-tuple-element.4), channel_id=1, replica_groups=mesh['row'=64,'pair'=8] {'row'}, use_global_device_ids=true, to_apply=%region_9.10 | all-reduce | flops 2048 | bytes 16384 | tf_op jit(solution)/shard_map/psum | solution.py:23
  432.3 0.1 multiply_add_fusion.3
  432.3 0.1 multiply_add_fusion.2
  432.4 0.0 all-gather.7.cloned.1.call-done
  432.5 9.9 fusion
  442.3 712.4 %all-reduce.4.cloned.1.call-done = (f32[512,512]{1,0:T(8,128)}, f32[512,512]{1,0:T(8,128)}) async-done(((f32[512,512]{1,0:T(8,128)}, f32[512,512]{1,0:T(8,128)}), (f32[512,512]{1,0:T(8,128)}, f32[512,512]{1,0:T(8,128)})) %all-reduce.4.cloned.1.call-update) | async-done | bytes 2097168 | tf_op jit(solution)/shard_map/psum | solution.py:23
  1154.8 0.8 divide_bitcast_fusion
  1155.6 0.6 maximum_bitcast_fusion
  (2 shorter events, 0.0 us)
Async XLA Ops:
  7.2 132.2 %all-gather.5.cloned.1.call-start = ((), (), s32[]{:S(2)}) async-start(), calls=%async_computation | async-start | bytes 4259840 | tf_op jit(solution)/shard_map/all_gather | solution.py:44
  8.8 423.7 %all-gather.7.cloned.1.call-start = ((), (), s32[]{:S(2)}) async-start(), calls=%async_computation.1 | async-start | bytes 4259840 | tf_op jit(solution)/shard_map/all_gather | solution.py:44
  9.5 1145.3 %all-reduce.4.cloned.1.call-start = ((), (), s32[]{:S(2)}) async-start(), calls=%async_computation.2 | async-start | bytes 4194304 | tf_op jit(solution)/shard_map/psum | solution.py:23
  149.0 2.1 copy-start.1
  149.0 6.6 copy-start
  151.1 25.7 %collective-permute-start = (f32[512,512]{1,0:T(8,128)}, f32[512,512]{1,0:T(8,128)S(1)}, u32[]{:S(2)}, u32[]{:S(2)}) collective-permute-start(f32[512,512]{1,0:T(8,128)} %get-tuple-element.18), channel_id=1, source_target_pairs={{0,1},{1,2},{2,3},{3,4},{4,5},{5,6},{6,7},{8,9},{9,10},{10,11},{11... | collective-permute-start | bytes 3145736 | tf_op jit(solution)/shard_map/ppermute | solution.py:12
  154.3 26.4 %collective-permute-start.1 = (f32[512,512]{1,0:T(8,128)}, f32[512,512]{1,0:T(8,128)}, u32[]{:S(2)}, u32[]{:S(2)}) collective-permute-start(f32[512,512]{1,0:T(8,128)} %get-tuple-element.19), channel_id=1, source_target_pairs={{1,0},{2,1},{3,2},{4,3},{5,4},{6,5},{7,6},{9,8},{10,9},{11,10},{12... | collective-permute-start | bytes 3145736 | tf_op jit(solution)/shard_map/ppermute | solution.py:12
  155.6 25.1 %copy-start.2 = (f32[512,1024]{1,0:T(8,128)S(1)}, f32[512,1024]{1,0:T(8,128)}, u32[]{:S(2)}) copy-start(f32[512,1024]{1,0:T(8,128)} %copy-done.1) | copy-start | bytes 6291460
  176.9 1.0 copy-start.4
  182.4 1.1 copy-start.3
Sparse Core Ops, SparseCore 0:
  10.7 128.5 all-gather.4
  141.5 179.3 all-gather.6
  323.8 830.9 all-reduce.3
where the time goes:
time: 1160 us
  waiting for transfers between devices  864 us (74%)
  blocking collectives  246 us (21%)
  matrix products  25.2 us (2%)
  between operations  13.8 us (1%)
    psum x1, waiting for transfers between devices, couple(): lax.psum((cross, jnp.sum(top * top, axis=0), jnp.sum(bottom * bottom, axi...  712 us
    psum x1, blocking collectives, couple(): lax.psum((cross, jnp.sum(top * top, axis=0), jnp.sum(bottom * bottom, axi...  246 us
    all_gather x2, waiting for transfers between devices, per_device(): transform = lax.all_gather(rotations[step, 0], 'row', axis=0, tiled=True)  130 us
  transfers between devices with their start and end apart: 5, of which 4 were waited for; matrix products, arithmetic and copies ran while one was open for 2% of the time, Pallas kernels for 0%

commit v1 on v0

v1 whole, which is shorter than its diff:
```python
import jax
import jax.numpy as jnp
from jax import lax
from jax.experimental import pallas as pl
from jax.experimental.pallas import tpu as pltpu
from jax.sharding import PartitionSpec as P

MESH = pl.DeviceIdType.MESH
F32 = jnp.float32
BF16 = jnp.bfloat16

YS, ZS, CS = 4, 8, 2
PAIRS = 8
B = 512
W = 2 * B
ROWS = 512
TOTAL = 32768
SHARE = 16
GROUP = 256
OFFSETS = (0, 512, 256, 768)
HALF = 512


def split(value):
    high = value.astype(BF16)
    return high, (value - high.astype(F32)).astype(BF16)


def dot3(a_high, a_low, b_high, b_low, dims):
    dot = lambda a, b: lax.dot_general(a, b, (dims, ((), ())), preferred_element_type=F32)
    return dot(a_high, b_high) + (dot(a_low, b_high) + dot(a_high, b_low))


def body(
    x_hbm, rot_ref, out_ref, coup_ref,
    x_ref, xh, xl, rg, staged, new, nh, nl,
    cx, nrm, rc, rcn, pb, pn, ry, ryn, qz, rz,
    x_sem, gs, gr, ms, mr, rs_s, rs_r,
):
    row = lax.axis_index("row")
    pair = lax.axis_index("pair")
    y = row // (ZS * CS)
    z = (row // CS) % ZS
    c = row % CS
    chip = y * ZS + z

    def at(yy, zz, cc):
        return ((yy * ZS + zz) * CS + cc, pair)

    sibling = at(y, z, 1 - c)
    after = (row, (pair + 1) % PAIRS)
    before = (row, (pair + PAIRS - 1) % PAIRS)
    y_other = [at((y + j) % YS, z, c) for j in range(1, YS)]
    z_other = [at(y, (z + j) % ZS, c) for j in range(1, ZS)]
    z_group = [at(y, (z // 4) * 4 + (z + j) % 4, c) for j in range(1, 4)]
    z_across = at(y, (z + 4) % ZS, c)

    pending = []

    def send(src, dst, s_sem, r_sem, device):
        copy = pltpu.make_async_remote_copy(
            src_ref=src, dst_ref=dst, send_sem=s_sem, recv_sem=r_sem,
            device_id=device, device_id_type=MESH,
        )
        copy.start()
        pending.append(copy)
        return copy

    x_copy = pltpu.make_async_copy(x_hbm, x_ref, x_sem)
    x_copy.start()

    barrier = pltpu.get_barrier_semaphore()
    partners = [sibling, after, before] + y_other + z_other
    for device in partners:
        pl.semaphore_signal(barrier, inc=1, device_id=device, device_id_type=MESH)
    own = pl.ds(pl.multiple_of(c * SHARE, SHARE), SHARE)
    for k in range(2):
        rg[k, pl.ds(chip, 1), own, :] = rot_ref[k]
    pl.semaphore_wait(barrier, len(partners))

    units = [(0, o, GROUP) for o in OFFSETS] + [(1, 0, HALF), (1, HALF, HALF)]
    waits = {}

    def gather_z1(u):
        k, o, n = units[u]
        ref = rg.at[k, pl.ds(chip, 1), own, pl.ds(o, n)]
        waits[u, "across"] = send(ref, ref, gs.at[u, 0], gr.at[u, 0], z_across)
        waits[u, "z1"] = [
            send(ref, ref, gs.at[u, 1 + j], gr.at[u, 1 + j], z_group[j]) for j in range(3)
        ]

    def gather_z2(u):
        k, o, n = units[u]
        waits[u, "across"].wait_recv()
        ref = rg.at[k, pl.ds(y * ZS + (z + 4) % ZS, 1), own, pl.ds(o, n)]
        waits[u, "z2"] = [
            send(ref, ref, gs.at[u, 4 + j], gr.at[u, 4 + j], z_group[j]) for j in range(3)
        ]

    def gather_y(u):
        k, o, n = units[u]
        for copy in waits[u, "z1"] + waits[u, "z2"]:
            copy.wait_recv()
        ref = rg.at[k, pl.ds(y * ZS, ZS), own, pl.ds(o, n)]
        waits[u, "y"] = [
            send(ref, ref, gs.at[u, 7 + j], gr.at[u, 7 + j], y_other[j]) for j in range(3)
        ]

    def gather_c(u):
        k, o, n = units[u]
        for copy in waits[u, "y"]:
            copy.wait_recv()
        ref = rg.at[k, :, own, pl.ds(o, n)]
        waits[u, "c"] = send(ref, ref, gs.at[u, 10], gr.at[u, 10], sibling)

    def gather_done(u):
        waits[u, "c"].wait_recv()

    def gram(k, high, low, top, bottom):
        for t in range(2):
            cols = slice(t * GROUP, (t + 1) * GROUP)
            tile = dot3(high[:, cols], low[:, cols], high[:, B:], low[:, B:], ((0,), (0,)))
            cx[k, 2 * t : 2 * t + 2] = tile.reshape(2, ZS, CS * 8, B)
        for i, ref in enumerate((top, bottom)):
            def add(step, total):
                part = ref[pl.ds(pl.multiple_of(step * 32, 32), 32), :]
                return total + jnp.sum((part * part).reshape(4, 8, B), axis=0)
            total = lax.fori_loop(0, ROWS // 32, add, jnp.zeros((8, B), F32))
            norm = jnp.sum(total, axis=0, keepdims=True)
            for j in range(4):
                nrm[k, 4 * i + j : 4 * i + j + 1, :] = norm[:, 128 * j : 128 * (j + 1)]

    mine = pl.ds(pl.multiple_of(c * 8, 8), 8)
    theirs = pl.ds(pl.multiple_of((1 - c) * 8, 8), 8)

    def reduce_c(k):
        waits[k, "rc"] = [
            send(cx.at[k, :, :, theirs, :], rc.at[k], rs_s.at[k, 0], rs_r.at[k, 0], sibling),
            send(nrm.at[k], rcn.at[k], rs_s.at[k, 1], rs_r.at[k, 1], sibling),
        ]

    def reduce_y(k):
        for copy in waits[k, "rc"]:
            copy.wait_recv()
        pb[k] = cx[k, :, :, mine, :] + rc[k]
        pn[k] = nrm[k] + rcn[k]
        waits[k, "ry"] = []
        for j in range(3):
            waits[k, "ry"] += [
                send(pb.at[k, (y + j + 1) % YS], ry.at[k, j], rs_s.at[k, 2 + j], rs_r.at[k, 2 + j], y_other[j]),
                send(pn.at[k], ryn.at[k, j], rs_s.at[k, 5 + j], rs_r.at[k, 5 + j], y_other[j]),
            ]

    def reduce_z(k):
        for copy in waits[k, "ry"]:
            copy.wait_recv()
        qz[k, :, :, :B] = pb[k, y] + ry[k, 0] + (ry[k, 1] + ry[k, 2])
        norms = pn[k] + ryn[k, 0] + (ryn[k, 1] + ryn[k, 2])
        for j in range(ZS):
            qz[k, j, :, B:] = norms
        waits[k, "rz"] = [
            send(qz.at[k, (z + j + 1) % ZS], rz.at[k, j], rs_s.at[k, 8 + j], rs_r.at[k, 8 + j], z_other[j])
            for j in range(7)
        ]

    def couple(k):
        for copy in waits[k, "rz"]:
            copy.wait_recv()
        total = qz[k, z]
        for j in range(7):
            total = total + rz[k, j]
        cross = total[:, :B]
        norms = total[:, B:]
        rows = [jnp.concatenate([norms[4 * i + j : 4 * i + j + 1, :] for j in range(4)], axis=1) for i in range(2)]
        mean_top = rows[0] / TOTAL + 1e-06
        mean_bottom = rows[1] / TOTAL + 1e-06
        here = lax.broadcasted_iota(jnp.int32, (8, B), 0) + 8 * row
        column = lax.broadcasted_iota(jnp.int32, (8, B), 1)
        mean_top = jnp.sum(jnp.where(here == column, mean_top, 0.0), axis=1, keepdims=True)
        scale = jnp.sqrt(F32(TOTAL)) * jnp.sqrt(mean_top * mean_bottom)
        coup_ref[k, 0] = cross / scale

    def turn(k, high, low, o):
        w = rg[k, :, :, o : o + GROUP].reshape(W, GROUP)
        w_high, w_low = split(w)
        return dot3(high[...], low[...], w_high, w_low, ((1,), (0,)))

    def move(g):
        src = staged.at[g]
        cols = pl.ds((g // 2) * GROUP, GROUP)
        sems = ms.at[g], mr.at[g]
        if g % 2 == 0:
            @pl.when(pair == 0)
            def _():
                new[0, :, cols] = src[...]

            @pl.when(pair == PAIRS - 1)
            def _():
                new[1, :, cols] = src[...]

            @pl.when((pair > 0) & (pair < PAIRS - 1))
            def _():
                up(g).start()
        else:
            @pl.when(pair == 0)
            def _():
                up(g).start()

            @pl.when(pair > 0)
            def _():
                down(g).start()

    def up(g):
        h = g // 2
        return pltpu.make_async_remote_copy(
            src_ref=staged.at[g], dst_ref=new.at[0, :, pl.ds(h * GROUP, GROUP)],
            send_sem=ms.at[g], recv_sem=mr.at[2 * h], device_id=after, device_id_type=MESH,
        )

    def down(g):
        h = g // 2
        return pltpu.make_async_remote_copy(
            src_ref=staged.at[g], dst_ref=new.at[1, :, pl.ds(h * GROUP, GROUP)],
            send_sem=ms.at[g], recv_sem=mr.at[2 * h + 1], device_id=before, device_id_type=MESH,
        )

    def arrived(g):
        if g % 2 == 0:
            @pl.when(pair > 0)
            def _():
                up(g).wait_recv()
        else:
            @pl.when(pair < PAIRS - 1)
            def _():
                down(g).wait_recv()
        i, h = g % 2, g // 2
        cols = slice(h * GROUP, (h + 1) * GROUP)
        into = slice(i * B + h * GROUP, i * B + (h + 1) * GROUP)
        nh[:, into], nl[:, into] = split(new[i, :, cols])

    def sent(g):
        if g % 2 == 0:
            @pl.when((pair > 0) & (pair < PAIRS - 1))
            def _():
                up(g).wait_send()
        else:
            @pl.when(pair == 0)
            def _():
                up(g).wait_send()

            @pl.when(pair > 0)
            def _():
                down(g).wait_send()

    for u in range(4):
        gather_z1(u)
    x_copy.wait()
    xh[...], xl[...] = split(x_ref[...])
    gram(0, xh, xl, x_ref.at[:, :B], x_ref.at[:, B:])

    def first(g):
        gather_done(g)
        staged[g] = turn(0, xh, xl, OFFSETS[g])
        move(g)

    gather_z2(0)
    gather_z2(1)
    gather_y(0)
    gather_z2(2)
    gather_y(1)
    gather_z2(3)
    gather_c(0)
    gather_y(2)
    first(0)
    gather_c(1)
    gather_y(3)
    gather_z1(4)
    gather_z1(5)
    first(1)
    gather_c(2)
    gather_z2(4)
    first(2)
    gather_z2(5)
    gather_c(3)
    gather_y(4)
    first(3)
    reduce_c(0)
    gather_y(5)
    reduce_y(0)
    gather_c(4)
    reduce_z(0)
    gather_c(5)
    couple(0)
    gather_done(4)
    gather_done(5)

    for g in range(4):
        arrived(g)
    gram(1, nh, nl, new.at[0], new.at[1])
    reduce_c(1)

    def second(g):
        out_ref[:, OFFSETS[g] : OFFSETS[g] + GROUP] = turn(1, nh, nl, OFFSETS[g])

    second(0)
    reduce_y(1)
    second(1)
    second(2)
    reduce_z(1)
    second(3)
    couple(1)
    for copy in pending:
        copy.wait_send()
    for g in range(4):
        sent(g)


def per_device(matrix, rotations):
    vmem = pl.BlockSpec(memory_space=pltpu.VMEM)
    scratch = [
        pltpu.VMEM((ROWS, W), F32),
        pltpu.VMEM((ROWS, W), BF16),
        pltpu.VMEM((ROWS, W), BF16),
        pltpu.VMEM((2, YS * ZS, CS * SHARE, W), F32),
        pltpu.VMEM((4, ROWS, GROUP), F32),
        pltpu.VMEM((2, ROWS, B), F32),
        pltpu.VMEM((ROWS, W), BF16),
        pltpu.VMEM((ROWS, W), BF16),
        pltpu.VMEM((2, YS, ZS, CS * 8, B), F32),
        pltpu.VMEM((2, 8, 128), F32),
        pltpu.VMEM((2, YS, ZS, 8, B), F32),
        pltpu.VMEM((2, 8, 128), F32),
        pltpu.VMEM((2, YS, ZS, 8, B), F32),
        pltpu.VMEM((2, 8, 128), F32),
        pltpu.VMEM((2, 3, ZS, 8, B), F32),
        pltpu.VMEM((2, 3, 8, 128), F32),
        pltpu.VMEM((2, ZS, 8, B + 128), F32),
        pltpu.VMEM((2, 7, 8, B + 128), F32),
        pltpu.SemaphoreType.DMA,
        pltpu.SemaphoreType.DMA((6, 11)),
        pltpu.SemaphoreType.DMA((6, 11)),
        pltpu.SemaphoreType.DMA((4,)),
        pltpu.SemaphoreType.DMA((4,)),
        pltpu.SemaphoreType.DMA((2, 15)),
        pltpu.SemaphoreType.DMA((2, 15)),
    ]
    return pl.pallas_call(
        body,
        name="tournament",
        out_shape=(
            jax.ShapeDtypeStruct((ROWS, W), F32),
            jax.ShapeDtypeStruct((2, 1, 8, B), F32),
        ),
        in_specs=[pl.BlockSpec(memory_space=pl.ANY), vmem],
        out_specs=(vmem, vmem),
        scratch_shapes=scratch,
        compiler_params=pltpu.CompilerParams(
            collective_id=0, has_side_effects=True, vmem_limit_bytes=56 << 20
        ),
    )(matrix, rotations)


def solution(mesh):
    specs = (P("row", "pair"), P(None, "pair", "row", None))
    return jax.shard_map(
        per_device, mesh=mesh, in_specs=specs, out_specs=specs, check_vma=False
    )
```

time: 1160 us -> 198 us (0.17)
  the two profiles are of different devices: /device:TPU:1 before, /device:TPU:6 now
where the time goes in v1:
time: 198 us
  Pallas kernels  194 us (98%)
  local copies, waits for them, and re-layouts  3.78 us (2%)
    pallas_call x1, Pallas kernels, per_device(): pl.pallas_call(body, name='tournament', out_shape=(jax.ShapeDtypeStruct((...  194 us

profile of v1, /device:TPU:6, one launch (start us, length us, event | category | flops | bytes accessed | tf_op | source)
XLA Modules:
  0.0 198.1 jit_solution(12873153801509947509)
XLA Ops:
  0.6 193.7 %tournament.1 = (f32[512,1024]{1,0:T(8,128)}, f32[2,1,8,512]{3,2,1,0:T(8,128)}) custom-call(f32[512,1024]{1,0:T(8,128)} %x_hbm.1, f32[2,1,16,1024]{3,2,1,0:T(8,128)} %rot_ref.1), custom_call_target="tpu_custom_call" | custom-call | tf_op jit(solution)/shard_map/tournament/pallas_call | solution.py:347
  194.3 0.0 copy-start
  194.3 3.2 %copy.6 = f32[512,1024]{1,0:T(8,128)} copy(f32[512,1024]{1,0:T(8,128)} %get-tuple-element.4) | data formatting | bytes 4194304
  197.5 0.0 copy-done
  197.5 0.6 copy.7
Async XLA Ops:
  194.3 3.2 %copy-start = (f32[2,1,8,512]{3,2,1,0:T(8,128)S(1)}, f32[2,1,8,512]{3,2,1,0:T(8,128)}, u32[]{:S(2)}) copy-start(f32[2,1,8,512]{3,2,1,0:T(8,128)} %get-tuple-element.5) | copy-start | bytes 98308

commit v2 on v1

--- a/solution.py
+++ b/solution.py
@@ -19,6 +19,7 @@
 GROUP = 256
 OFFSETS = (0, 512, 256, 768)
 HALF = 512
+QUARTER = 128
 
 
 def split(value):
@@ -35,7 +36,7 @@
     x_hbm, rot_ref, out_ref, coup_ref,
     x_ref, xh, xl, rg, staged, new, nh, nl,
     cx, nrm, rc, rcn, pb, pn, ry, ryn, qz, rz,
-    x_sem, gs, gr, ms, mr, rs_s, rs_r,
+    passing, x_sem, gs, gr, ms, mr, rs_s, rs_r, cs, cr, ps, pr,
 ):
     row = lax.axis_index("row")
     pair = lax.axis_index("pair")
@@ -48,8 +49,8 @@
         return ((yy * ZS + zz) * CS + cc, pair)
 
     sibling = at(y, z, 1 - c)
-    after = (row, (pair + 1) % PAIRS)
-    before = (row, (pair + PAIRS - 1) % PAIRS)
+    pair_other = [(row, (pair + j) % PAIRS) for j in range(1, PAIRS)]
+    after, before = pair_other[0], pair_other[-1]
     y_other = [at((y + j) % YS, z, c) for j in range(1, YS)]
     z_other = [at(y, (z + j) % ZS, c) for j in range(1, ZS)]
     z_group = [at(y, (z // 4) * 4 + (z + j) % 4, c) for j in range(1, 4)]
@@ -70,7 +71,7 @@
     x_copy.start()
 
     barrier = pltpu.get_barrier_semaphore()
-    partners = [sibling, after, before] + y_other + z_other
+    partners = [sibling] + pair_other + y_other + z_other
     for device in partners:
         pl.semaphore_signal(barrier, inc=1, device_id=device, device_id_type=MESH)
     own = pl.ds(pl.multiple_of(c * SHARE, SHARE), SHARE)
@@ -97,21 +98,30 @@
             send(ref, ref, gs.at[u, 4 + j], gr.at[u, 4 + j], z_group[j]) for j in range(3)
         ]
 
-    def gather_y(u):
+    def gather_y1(u):
         k, o, n = units[u]
         for copy in waits[u, "z1"] + waits[u, "z2"]:
             copy.wait_recv()
         ref = rg.at[k, pl.ds(y * ZS, ZS), own, pl.ds(o, n)]
-        waits[u, "y"] = [
-            send(ref, ref, gs.at[u, 7 + j], gr.at[u, 7 + j], y_other[j]) for j in range(3)
+        waits[u, "y1"] = [
+            send(ref, ref, gs.at[u, 7 + j], gr.at[u, 7 + j], y_other[2 * j]) for j in range(2)
         ]
+
+    def gather_y2(u):
+        k, o, n = units[u]
+        waits[u, "y2"] = []
+        for j in range(2):
+            waits[u, "y1"][j].wait_recv()
+            first = ((y + (3, 1)[j]) % YS) * ZS + j * (ZS // 2)
+            ref = rg.at[k, pl.ds(first, ZS // 2), own, pl.ds(o, n)]
+            waits[u, "y2"].append(send(ref, ref, gs.at[u, 9 + j], gr.at[u, 9 + j], y_other[2 * j]))
 
     def gather_c(u):
         k, o, n = units[u]
-        for copy in waits[u, "y"]:
+        for copy in waits[u, "y2"]:
             copy.wait_recv()
         ref = rg.at[k, :, own, pl.ds(o, n)]
-        waits[u, "c"] = send(ref, ref, gs.at[u, 10], gr.at[u, 10], sibling)
+        waits[u, "c"] = send(ref, ref, gs.at[u, 11], gr.at[u, 11], sibling)
 
     def gather_done(u):
         waits[u, "c"].wait_recv()
@@ -185,10 +195,22 @@
         w_high, w_low = split(w)
         return dot3(high[...], low[...], w_high, w_low, ((1,), (0,)))
 
+    def is_up(g):
+        if g % 2 == 1:
+            return pair == 0
+        return (pair > 0) & (pair < PAIRS - 1) & (pair != 3)
+
+    def is_down(g):
+        return (pair > 0) & (pair != 4) if g % 2 == 1 else None
+
     def move(g):
         src = staged.at[g]
         cols = pl.ds((g // 2) * GROUP, GROUP)
-        sems = ms.at[g], mr.at[g]
+
+        @pl.when(is_up(g))
+        def _():
+            up(g).start()
+
         if g % 2 == 0:
             @pl.when(pair == 0)
             def _():
@@ -197,18 +219,39 @@
             @pl.when(pair == PAIRS - 1)
             def _():
                 new[1, :, cols] = src[...]
-
-            @pl.when((pair > 0) & (pair < PAIRS - 1))
-            def _():
-                up(g).start()
         else:
-            @pl.when(pair == 0)
-            def _():
-                up(g).start()
-
-            @pl.when(pair > 0)
+            @pl.when(is_down(g))
             def _():
                 down(g).start()
+
+        @pl.when(pair == 3 + g % 2)
+        def _():
+            for j in range(4):
+                far(g, j).start()
+
+    def far(g, j):
+        i, h = g % 2, g // 2
+        rows = pl.ds(j * QUARTER, QUARTER)
+        dst = new.at[i, rows, pl.ds(h * GROUP, GROUP)] if j == 0 else passing.at[h]
+        to = 4 - i if j == 0 else (3 - j, 4 + j)[i]
+        return pltpu.make_async_remote_copy(
+            src_ref=staged.at[g, rows], dst_ref=dst, send_sem=cs.at[h, j],
+            recv_sem=cr.at[h, 0] if j == 0 else pr.at[h], device_id=(row, to), device_id_type=MESH,
+        )
+
+    def passed(g, j):
+        i, h = g % 2, g // 2
+        return pltpu.make_async_remote_copy(
+            src_ref=passing.at[h], dst_ref=new.at[i, pl.ds(j * QUARTER, QUARTER), pl.ds(h * GROUP, GROUP)],
+            send_sem=ps.at[h], recv_sem=cr.at[h, j], device_id=(row, 4 - i), device_id_type=MESH,
+        )
+
+    def pass_on(g):
+        for j in range(1, 4):
+            @pl.when(pair == (3 - j, 4 + j)[g % 2])
+            def _():
+                far(g, j).wait_recv()
+                passed(g, j).start()
 
     def up(g):
         h = g // 2
@@ -225,87 +268,111 @@
         )
 
     def arrived(g):
-        if g % 2 == 0:
-            @pl.when(pair > 0)
+        i, h = g % 2, g // 2
+        if i == 0:
+            @pl.when((pair > 0) & (pair != 4))
             def _():
                 up(g).wait_recv()
         else:
-            @pl.when(pair < PAIRS - 1)
+            @pl.when((pair < PAIRS - 1) & (pair != 3))
             def _():
                 down(g).wait_recv()
-        i, h = g % 2, g // 2
+
+        @pl.when(pair == 4 - i)
+        def _():
+            far(g, 0).wait_recv()
+            for j in range(1, 4):
+                passed(g, j).wait_recv()
+
         cols = slice(h * GROUP, (h + 1) * GROUP)
         into = slice(i * B + h * GROUP, i * B + (h + 1) * GROUP)
         nh[:, into], nl[:, into] = split(new[i, :, cols])
 
     def sent(g):
-        if g % 2 == 0:
-            @pl.when((pair > 0) & (pair < PAIRS - 1))
-            def _():
-                up(g).wait_send()
-        else:
-            @pl.when(pair == 0)
-            def _():
-                up(g).wait_send()
-
-            @pl.when(pair > 0)
+        @pl.when(is_up(g))
+        def _():
+            up(g).wait_send()
+
+        if g % 2 == 1:
+            @pl.when(is_down(g))
             def _():
                 down(g).wait_send()
 
-    for u in range(4):
-        gather_z1(u)
-    x_copy.wait()
-    xh[...], xl[...] = split(x_ref[...])
-    gram(0, xh, xl, x_ref.at[:, :B], x_ref.at[:, B:])
+        @pl.when(pair == 3 + g % 2)
+        def _():
+            for j in range(4):
+                far(g, j).wait_send()
+
+        for j in range(1, 4):
+            @pl.when(pair == (3 - j, 4 + j)[g % 2])
+            def _():
+                passed(g, j).wait_send()
 
     def first(g):
         gather_done(g)
         staged[g] = turn(0, xh, xl, OFFSETS[g])
         move(g)
 
+    def second(g):
+        out_ref[:, OFFSETS[g] : OFFSETS[g] + GROUP] = turn(1, nh, nl, OFFSETS[g])
+
+    gather_z1(0)
+    gather_z1(1)
+    x_copy.wait()
+    xh[...], xl[...] = split(x_ref[...])
+    gram(0, xh, xl, x_ref.at[:, :B], x_ref.at[:, B:])
+    reduce_c(0)
     gather_z2(0)
+    gather_z1(2)
     gather_z2(1)
-    gather_y(0)
+    gather_z1(3)
+    reduce_y(0)
+    gather_y1(0)
     gather_z2(2)
-    gather_y(1)
+    gather_y1(1)
     gather_z2(3)
+    gather_y2(0)
+    gather_y1(2)
+    gather_z1(4)
+    gather_z1(5)
     gather_c(0)
-    gather_y(2)
+    gather_y2(1)
+    gather_y1(3)
     first(0)
     gather_c(1)
-    gather_y(3)
-    gather_z1(4)
-    gather_z1(5)
+    gather_y2(2)
+    reduce_z(0)
     first(1)
+    pass_on(0)
     gather_c(2)
+    gather_y2(3)
     gather_z2(4)
+    gather_z2(5)
     first(2)
-    gather_z2(5)
+    pass_on(1)
     gather_c(3)
-    gather_y(4)
+    gather_y1(4)
     first(3)
-    reduce_c(0)
-    gather_y(5)
-    reduce_y(0)
+    pass_on(2)
+    gather_y2(4)
+    gather_y1(5)
+    pass_on(3)
+    couple(0)
+    arrived(0)
     gather_c(4)
-    reduce_z(0)
+    gather_y2(5)
+    arrived(1)
+    arrived(2)
     gather_c(5)
-    couple(0)
-    gather_done(4)
-    gather_done(5)
-
-    for g in range(4):
-        arrived(g)
+    arrived(3)
     gram(1, nh, nl, new.at[0], new.at[1])
     reduce_c(1)
-
-    def second(g):
-        out_ref[:, OFFSETS[g] : OFFSETS[g] + GROUP] = turn(1, nh, nl, OFFSETS[g])
-
+    gather_done(4)
     second(0)
     reduce_y(1)
+    second(2)
+    gather_done(5)
     second(1)
-    second(2)
     reduce_z(1)
     second(3)
     couple(1)
@@ -336,13 +403,18 @@
         pltpu.VMEM((2, 3, 8, 128), F32),
         pltpu.VMEM((2, ZS, 8, B + 128), F32),
         pltpu.VMEM((2, 7, 8, B + 128), F32),
+        pltpu.VMEM((2, QUARTER, GROUP), F32),
         pltpu.SemaphoreType.DMA,
-        pltpu.SemaphoreType.DMA((6, 11)),
-        pltpu.SemaphoreType.DMA((6, 11)),
+        pltpu.SemaphoreType.DMA((6, 12)),
+        pltpu.SemaphoreType.DMA((6, 12)),
         pltpu.SemaphoreType.DMA((4,)),
         pltpu.SemaphoreType.DMA((4,)),
         pltpu.SemaphoreType.DMA((2, 15)),
         pltpu.SemaphoreType.DMA((2, 15)),
+        pltpu.SemaphoreType.DMA((2, 4)),
+        pltpu.SemaphoreType.DMA((2, 4)),
+        pltpu.SemaphoreType.DMA((2,)),
+        pltpu.SemaphoreType.DMA((2,)),
     ]
     return pl.pallas_call(
         body,

time: 198 us -> 121 us (0.61)
  the two profiles are of different devices: /device:TPU:6 before, /device:TPU:1 now
where the time goes in v2:
time: 121 us; the launch traced here: 118 us
  Pallas kernels  114 us (94%)
  local copies, waits for them, and re-layouts  3.78 us (3%)
    pallas_call x1, Pallas kernels, per_device(): pl.pallas_call(body, name='tournament', out_shape=(jax.ShapeDtypeStruct((...  114 us
    unnamed x4, local copies, waits for them, and re-layouts  3.78 us

profile of v2, /device:TPU:1, one launch (start us, length us, event | category | flops | bytes accessed | tf_op | source)
XLA Modules:
  0.0 118.4 jit_solution(12385246516334288889)
XLA Ops:
  0.6 114.0 %tournament.1 = (f32[512,1024]{1,0:T(8,128)}, f32[2,1,8,512]{3,2,1,0:T(8,128)}) custom-call(f32[512,1024]{1,0:T(8,128)} %x_hbm.1, f32[2,1,16,1024]{3,2,1,0:T(8,128)} %rot_ref.1), custom_call_target="tpu_custom_call" | custom-call | tf_op jit(solution)/shard_map/tournament/pallas_call | solution.py:419
  114.6 0.0 copy-start
  114.6 3.2 %copy.6 = f32[512,1024]{1,0:T(8,128)} copy(f32[512,1024]{1,0:T(8,128)} %get-tuple-element.4) | data formatting | bytes 4194304
  117.8 0.0 copy-done
  117.8 0.6 copy.7
Async XLA Ops:
  114.6 3.2 %copy-start = (f32[2,1,8,512]{3,2,1,0:T(8,128)S(1)}, f32[2,1,8,512]{3,2,1,0:T(8,128)}, u32[]{:S(2)}) copy-start(f32[2,1,8,512]{3,2,1,0:T(8,128)} %get-tuple-element.5) | copy-start | bytes 98308

commit v3 on v2

v3 whole, which is shorter than its diff:
```python
import jax
import jax.numpy as jnp
from jax import lax
from jax.experimental import pallas as pl
from jax.experimental.pallas import tpu as pltpu
from jax.sharding import PartitionSpec as P

MESH = pl.DeviceIdType.MESH
F32 = jnp.float32
BF16 = jnp.bfloat16

YS, ZS, CS = 4, 8, 2
PAIRS = 8
B = 512
W = 2 * B
ROWS = 512
TOTAL = 32768
SHARE = 16
GROUP = 256
PART = 128
HALF = 512
SHARES = ((0, 144), (144, 112), (256, 112), (368, 144))


def split(value):
    high = value.astype(BF16)
    return high, (value - high.astype(F32)).astype(BF16)


def dot3(a_high, a_low, b_high, b_low, dims):
    dot = lambda a, b: lax.dot_general(a, b, (dims, ((), ())), preferred_element_type=F32)
    return dot(a_high, b_high) + (dot(a_low, b_high) + dot(a_high, b_low))


def body(
    x_hbm, rot_ref, out_ref, coup_ref,
    x_ref, xh, xl, rg, staged, new, nh, nl,
    cx, nrm, rc, rcn, pb, pn, ry, ryn, qz, rz,
    passing, x_sem, gs, gr, ms, mr, rs_s, rs_r, cs, cr, ps, pr,
):
    row = lax.axis_index("row")
    pair = lax.axis_index("pair")
    y = row // (ZS * CS)
    z = (row // CS) % ZS
    c = row % CS
    chip = y * ZS + z

    def at(yy, zz, cc):
        return ((yy * ZS + zz) * CS + cc, pair)

    sibling = at(y, z, 1 - c)
    pair_other = [(row, (pair + j) % PAIRS) for j in range(1, PAIRS)]
    after, before = pair_other[0], pair_other[-1]
    y_other = [at((y + j) % YS, z, c) for j in range(1, YS)]
    z_other = [at(y, (z + j) % ZS, c) for j in range(1, ZS)]
    z_group = [at(y, (z // 4) * 4 + (z + j) % 4, c) for j in range(1, 4)]
    z_across = at(y, (z + 4) % ZS, c)

    pending = []

    def send(src, dst, s_sem, r_sem, device):
        copy = pltpu.make_async_remote_copy(
            src_ref=src, dst_ref=dst, send_sem=s_sem, recv_sem=r_sem,
            device_id=device, device_id_type=MESH,
        )
        copy.start()
        pending.append(copy)
        return copy

    x_copy = pltpu.make_async_copy(x_hbm, x_ref, x_sem)
    x_copy.start()

    barrier = pltpu.get_barrier_semaphore()
    partners = [sibling] + pair_other + y_other + z_other
    for device in partners:
        pl.semaphore_signal(barrier, inc=1, device_id=device, device_id_type=MESH)
    own = pl.ds(pl.multiple_of(c * SHARE, SHARE), SHARE)
    for u in range(4):
        for i in range(2):
            first_column = i * B + u * PART
            rg[0, pl.ds(chip, 1), own, u * GROUP + i * PART : u * GROUP + (i + 1) * PART] = rot_ref[
                0, :, :, first_column : first_column + PART
            ]
    rg[1, pl.ds(chip, 1), own, :] = rot_ref[1]
    pl.semaphore_wait(barrier, len(partners))

    units = [(0, 0, PART), (0, PART, PART)] + [(0, g * GROUP, GROUP) for g in range(1, 4)]
    units += [(1, 0, HALF), (1, HALF, HALF)]
    narrow = 2
    waits = {}

    def gather_z1(u):
        k, o, n = units[u]
        ref = rg.at[k, pl.ds(chip, 1), own, pl.ds(o, n)]
        waits[u, "across"] = send(ref, ref, gs.at[u, 0], gr.at[u, 0], z_across)
        waits[u, "z1"] = [
            send(ref, ref, gs.at[u, 1 + j], gr.at[u, 1 + j], z_group[j]) for j in range(3)
        ]

    def gather_z2(u):
        k, o, n = units[u]
        waits[u, "across"].wait_recv()
        ref = rg.at[k, pl.ds(y * ZS + (z + 4) % ZS, 1), own, pl.ds(o, n)]
        waits[u, "z2"] = [
            send(ref, ref, gs.at[u, 4 + j], gr.at[u, 4 + j], z_group[j]) for j in range(3)
        ]

    def gather_y1(u):
        k, o, n = units[u]
        for copy in waits[u, "z1"] + waits[u, "z2"]:
            copy.wait_recv()
        ref = rg.at[k, pl.ds(y * ZS, ZS), own, pl.ds(o, n)]
        waits[u, "y1"] = [
            send(ref, ref, gs.at[u, 7 + j], gr.at[u, 7 + j], y_other[2 * j]) for j in range(2)
        ]
        if u < narrow:
            waits[u, "y2"] = waits[u, "y1"] + [send(ref, ref, gs.at[u, 9], gr.at[u, 9], y_other[1])]

    def gather_y2(u):
        k, o, n = units[u]
        waits[u, "y2"] = []
        for j in range(2):
            waits[u, "y1"][j].wait_recv()
            first = ((y + (3, 1)[j]) % YS) * ZS + j * (ZS // 2)
            ref = rg.at[k, pl.ds(first, ZS // 2), own, pl.ds(o, n)]
            waits[u, "y2"].append(send(ref, ref, gs.at[u, 9 + j], gr.at[u, 9 + j], y_other[2 * j]))

    def gather_c(u):
        k, o, n = units[u]
        for copy in waits[u, "y2"]:
            copy.wait_recv()
        ref = rg.at[k, :, own, pl.ds(o, n)]
        waits[u, "c"] = send(ref, ref, gs.at[u, 11], gr.at[u, 11], sibling)

    def gather_done(u):
        waits[u, "c"].wait_recv()

    def gram(k, high, low, o, n):
        tile = dot3(high[:, :B], low[:, :B], high[:, B + o : B + o + n], low[:, B + o : B + o + n], ((0,), (0,)))
        cx[k, :, :, :, o : o + n] = tile.reshape(YS, ZS, CS * 8, n)

    def norms(k, top, bottom):
        for i, ref in enumerate((top, bottom)):
            def add(step, total):
                part = ref[pl.ds(pl.multiple_of(step * 32, 32), 32), :]
                return total + jnp.sum((part * part).reshape(4, 8, B), axis=0)
            total = lax.fori_loop(0, ROWS // 32, add, jnp.zeros((8, B), F32))
            norm = jnp.sum(total, axis=0, keepdims=True)
            for j in range(4):
                nrm[k, 4 * i + j : 4 * i + j + 1, :] = norm[:, 128 * j : 128 * (j + 1)]

    mine = pl.ds(pl.multiple_of(c * 8, 8), 8)
    theirs = pl.ds(pl.multiple_of((1 - c) * 8, 8), 8)
    parts = [(0, 0, B), (1, 0, GROUP), (1, GROUP, GROUP)]

    def reduce_c(q):
        k, o, n = parts[q]
        cols = pl.ds(o, n)
        waits[q, "rc"] = [
            send(cx.at[k, :, :, theirs, cols], rc.at[k, :, :, :, cols], rs_s.at[q, 0], rs_r.at[q, 0], sibling)
        ]
        if o == 0:
            waits[q, "rc"].append(send(nrm.at[k], rcn.at[k], rs_s.at[q, 1], rs_r.at[q, 1], sibling))

    def reduce_y(q):
        k, o, n = parts[q]
        cols = pl.ds(o, n)
        for copy in waits[q, "rc"]:
            copy.wait_recv()
        pb[k, :, :, :, cols] = cx[k, :, :, mine, cols] + rc[k, :, :, :, cols]
        if o == 0:
            pn[k] = nrm[k] + rcn[k]
        waits[q, "ry"] = []
        for j in range(3):
            waits[q, "ry"].append(
                send(
                    pb.at[k, (y + j + 1) % YS, :, :, cols], ry.at[k, j, :, :, cols],
                    rs_s.at[q, 2 + j], rs_r.at[q, 2 + j], y_other[j],
                )
            )
            if o == 0:
                waits[q, "ry"].append(send(pn.at[k], ryn.at[k, j], rs_s.at[q, 5 + j], rs_r.at[q, 5 + j], y_other[j]))

    def reduce_z(q):
        k, o, n = parts[q]
        cols = pl.ds(o, n)
        for copy in waits[q, "ry"]:
            copy.wait_recv()
        get = lambda ref, j: ref[k, j, :, :, cols]
        qz[k, :, :, 128 + o : 128 + o + n] = get(pb, y) + get(ry, 0) + (get(ry, 1) + get(ry, 2))
        if o == 0:
            total = pn[k] + ryn[k, 0] + (ryn[k, 1] + ryn[k, 2])
            for j in range(ZS):
                qz[k, j, :, :128] = total
        with_norms = pl.ds(0, n + 128) if o == 0 else pl.ds(o + 128, n)
        waits[q, "rz"] = [
            send(
                qz.at[k, (z + j + 1) % ZS, :, with_norms], rz.at[k, j, :, with_norms],
                rs_s.at[q, 8 + j], rs_r.at[q, 8 + j], z_other[j],
            )
            for j in range(7)
        ]

    def couple(k):
        for q in range(3):
            if parts[q][0] == k:
                for copy in waits[q, "rz"]:
                    copy.wait_recv()
        total = qz[k, z]
        for j in range(7):
            total = total + rz[k, j]
        cross = total[:, 128:]
        norm = total[:, :128]
        rows = [jnp.concatenate([norm[4 * i + j : 4 * i + j + 1, :] for j in range(4)], axis=1) for i in range(2)]
        mean_top = rows[0] / TOTAL + 1e-06
        mean_bottom = rows[1] / TOTAL + 1e-06
        here = lax.broadcasted_iota(jnp.int32, (8, B), 0) + 8 * row
        column = lax.broadcasted_iota(jnp.int32, (8, B), 1)
        mean_top = jnp.sum(jnp.where(here == column, mean_top, 0.0), axis=1, keepdims=True)
        scale = jnp.sqrt(F32(TOTAL)) * jnp.sqrt(mean_top * mean_bottom)
        coup_ref[k, 0] = cross / scale

    def turn(k, high, low, o, n):
        w = rg[k, :, :, o : o + n].reshape(W, n)
        w_high, w_low = split(w)
        return dot3(high[...], low[...], w_high, w_low, ((1,), (0,)))

    tops_up = (pair > 0) & (pair < PAIRS - 1) & (pair != 3)
    bottoms_down = (pair > 0) & (pair != 4)

    def up(g, i):
        return pltpu.make_async_remote_copy(
            src_ref=staged.at[g, :, pl.ds(i * PART, PART)], dst_ref=new.at[0, :, pl.ds(g * PART, PART)],
            send_sem=ms.at[g, i], recv_sem=mr.at[g, 0], device_id=after, device_id_type=MESH,
        )

    def down(g):
        return pltpu.make_async_remote_copy(
            src_ref=staged.at[g, :, pl.ds(PART, PART)], dst_ref=new.at[1, :, pl.ds(g * PART, PART)],
            send_sem=ms.at[g, 1], recv_sem=mr.at[g, 1], device_id=before, device_id_type=MESH,
        )

    def far(g, i, j):
        rows = pl.ds(*SHARES[j])
        return pltpu.make_async_remote_copy(
            src_ref=staged.at[g, rows, pl.ds(i * PART, PART)],
            dst_ref=new.at[i, rows, pl.ds(g * PART, PART)] if j == 0 else passing.at[g, pl.ds(0, SHARES[j][1])],
            send_sem=cs.at[g, j], recv_sem=cr.at[g, 0] if j == 0 else pr.at[g],
            device_id=(row, 4 - i if j == 0 else (3 - j, 4 + j)[i]), device_id_type=MESH,
        )

    def passed(g, i, j):
        return pltpu.make_async_remote_copy(
            src_ref=passing.at[g, pl.ds(0, SHARES[j][1])], dst_ref=new.at[i, pl.ds(*SHARES[j]), pl.ds(g * PART, PART)],
            send_sem=ps.at[g], recv_sem=cr.at[g, j], device_id=(row, 4 - i), device_id_type=MESH,
        )

    def move(g, i):
        @pl.when(pair == 3 + i)
        def _():
            for j in (1, 2, 3, 0):
                far(g, i, j).start()

        if i == 0:
            @pl.when(tops_up)
            def _():
                up(g, 0).start()
        else:
            @pl.when(pair == 0)
            def _():
                up(g, 1).start()

            @pl.when(bottoms_down)
            def _():
                down(g).start()

        if i == 0:
            for p in (0, PAIRS - 1):
                @pl.when(pair == p)
                def _():
                    new[p // (PAIRS - 1), :, g * PART : (g + 1) * PART] = staged[g, :, :PART]

    def pass_on(g):
        for i in range(2):
            for j in range(1, 4):
                @pl.when(pair == (3 - j, 4 + j)[i])
                def _():
                    far(g, i, j).wait_recv()
                    passed(g, i, j).start()

    def arrived(g):
        @pl.when((pair > 0) & (pair != 4))
        def _():
            up(g, 0).wait_recv()

        @pl.when((pair < PAIRS - 1) & (pair != 3))
        def _():
            down(g).wait_recv()

        for i in range(2):
            @pl.when(pair == 4 - i)
            def _():
                far(g, i, 0).wait_recv()
                for j in range(1, 4):
                    passed(g, i, j).wait_recv()

            cols = slice(g * PART, (g + 1) * PART)
            into = slice(i * B + g * PART, i * B + (g + 1) * PART)
            nh[:, into], nl[:, into] = split(new[i, :, cols])

    def sent(g):
        for i in range(2):
            @pl.when(pair == 3 + i)
            def _():
                for j in range(4):
                    far(g, i, j).wait_send()

            for j in range(1, 4):
                @pl.when(pair == (3 - j, 4 + j)[i])
                def _():
                    passed(g, i, j).wait_send()

        @pl.when(tops_up)
        def _():
            up(g, 0).wait_send()

        @pl.when(pair == 0)
        def _():
            up(g, 1).wait_send()

        @pl.when(bottoms_down)
        def _():
            down(g).wait_send()

    def first(u):
        gather_done(u)
        _, o, n = units[u]
        g, start = o // GROUP, o % GROUP
        staged[g, :, start : start + n] = turn(0, xh, xl, o, n)
        for i in range(start // PART, (start + n) // PART):
            move(g, i)

    def second(g):
        out_ref[:, g * GROUP : (g + 1) * GROUP] = turn(1, nh, nl, g * GROUP, GROUP)

    gather_z1(0)
    gather_z1(1)
    gather_z1(2)
    x_copy.wait()
    xh[...], xl[...] = split(x_ref[...])
    norms(0, x_ref.at[:, :B], x_ref.at[:, B:])
    gram(0, xh, xl, 0, B)
    reduce_c(0)
    gather_z2(0)
    gather_z2(1)
    gather_z1(3)
    gather_z1(4)
    gather_z2(2)
    gather_y1(0)
    gather_y1(1)
    gather_z2(3)
    gather_y1(2)
    gather_z2(4)
    gather_c(0)
    gather_c(1)
    gather_z1(5)
    gather_z1(6)
    gather_y2(2)
    gather_y1(3)
    first(0)
    first(1)
    gather_y1(4)
    gather_c(2)
    gather_y2(3)
    gather_z2(5)
    pass_on(0)
    first(2)
    gather_y2(4)
    reduce_y(0)
    gather_c(3)
    gather_z2(6)
    first(3)
    pass_on(1)
    gather_c(4)
    first(4)
    gather_y1(5)
    pass_on(2)
    pass_on(3)
    gather_y1(6)
    gather_y2(5)
    gather_y2(6)
    arrived(0)
    arrived(1)
    arrived(2)
    arrived(3)
    norms(1, new.at[0], new.at[1])
    gram(1, nh, nl, 0, GROUP)
    reduce_c(1)
    gram(1, nh, nl, GROUP, GROUP)
    reduce_c(2)
    gather_c(5)
    reduce_z(0)
    reduce_y(1)
    reduce_y(2)
    gather_c(6)
    gather_done(5)
    second(0)
    second(1)
    reduce_z(1)
    reduce_z(2)
    gather_done(6)
    second(2)
    second(3)
    couple(0)
    couple(1)
    for copy in pending:
        copy.wait_send()
    for g in range(4):
        sent(g)


def per_device(matrix, rotations):
    vmem = pl.BlockSpec(memory_space=pltpu.VMEM)
    scratch = [
        pltpu.VMEM((ROWS, W), F32),
        pltpu.VMEM((ROWS, W), BF16),
        pltpu.VMEM((ROWS, W), BF16),
        pltpu.VMEM((2, YS * ZS, CS * SHARE, W), F32),
        pltpu.VMEM((4, ROWS, GROUP), F32),
        pltpu.VMEM((2, ROWS, B), F32),
        pltpu.VMEM((ROWS, W), BF16),
        pltpu.VMEM((ROWS, W), BF16),
        pltpu.VMEM((2, YS, ZS, CS * 8, B), F32),
        pltpu.VMEM((2, 8, 128), F32),
        pltpu.VMEM((2, YS, ZS, 8, B), F32),
        pltpu.VMEM((2, 8, 128), F32),
        pltpu.VMEM((2, YS, ZS, 8, B), F32),
        pltpu.VMEM((2, 8, 128), F32),
        pltpu.VMEM((2, 3, ZS, 8, B), F32),
        pltpu.VMEM((2, 3, 8, 128), F32),
        pltpu.VMEM((2, ZS, 8, B + 128), F32),
        pltpu.VMEM((2, 7, 8, B + 128), F32),
        pltpu.VMEM((4, SHARES[0][1], PART), F32),
        pltpu.SemaphoreType.DMA,
        pltpu.SemaphoreType.DMA((7, 12)),
        pltpu.SemaphoreType.DMA((7, 12)),
        pltpu.SemaphoreType.DMA((4, 2)),
        pltpu.SemaphoreType.DMA((4, 2)),
        pltpu.SemaphoreType.DMA((3, 15)),
        pltpu.SemaphoreType.DMA((3, 15)),
        pltpu.SemaphoreType.DMA((4, 4)),
        pltpu.SemaphoreType.DMA((4, 4)),
        pltpu.SemaphoreType.DMA((4,)),
        pltpu.SemaphoreType.DMA((4,)),
    ]
    return pl.pallas_call(
        body,
        name="tournament",
        out_shape=(
            jax.ShapeDtypeStruct((ROWS, W), F32),
            jax.ShapeDtypeStruct((2, 1, 8, B), F32),
        ),
        in_specs=[pl.BlockSpec(memory_space=pl.ANY), vmem],
        out_specs=(vmem, vmem),
        scratch_shapes=scratch,
        compiler_params=pltpu.CompilerParams(
            collective_id=0, has_side_effects=True, vmem_limit_bytes=36 << 20
        ),
    )(matrix, rotations)


def solution(mesh):
    specs = (P("row", "pair"), P(None, "pair", "row", None))
    return jax.shard_map(
        per_device, mesh=mesh, in_specs=specs, out_specs=specs, check_vma=False
    )
```

time: 121 us -> 116 us (0.959); the launches traced: 118 us -> 115 us
  Pallas kernels: 114 us -> 110 us
    pallas_call x1, Pallas kernels: 114 us -> 110 us  [per_device(): pl.pallas_call(body, name='tournament', out_shape=(jax.ShapeDtypeStruct((...]
    unnamed x4 -> x6, local copies, waits for them, and re-layouts: 3.78 us -> 4.42 us
where the time goes in v3:
time: 116 us; the launch traced here: 115 us
  Pallas kernels  110 us (95%)
  local copies, waits for them, and re-layouts  4.42 us (4%)
    pallas_call x1, Pallas kernels, per_device(): pl.pallas_call(body, name='tournament', out_shape=(jax.ShapeDtypeStruct((...  110 us
    unnamed x6, local copies, waits for them, and re-layouts  4.42 us

profile of v3, /device:TPU:1, one launch (start us, length us, event | category | flops | bytes accessed | tf_op | source)
XLA Modules:
  0.0 115.5 jit_solution(14780160472898065762)
XLA Ops:
  0.6 0.0 copy-start
  0.6 1.6 %copy-done = f32[512,1024]{1,0:T(8,128)S(1)} copy-done((f32[512,1024]{1,0:T(8,128)S(1)}, f32[512,1024]{1,0:T(8,128)}, u32[]{:S(2)}) %copy-start) | copy-done | bytes 2097176
  2.2 0.0 copy-start.1
  2.2 0.9 copy-done.1
  3.1 110.4 %tournament.1 = (f32[512,1024]{1,0:T(8,128)S(1)}, f32[2,1,8,512]{3,2,1,0:T(8,128)S(1)}) custom-call(f32[512,1024]{1,0:T(8,128)S(1)} %copy-done, f32[2,1,16,1024]{3,2,1,0:T(8,128)S(1)} %copy-done.1), custom_call_target="tpu_custom_call" | custom-call | tf_op jit(solution)/shard_map/tournament/pallas_call | solution.py:456
  113.6 1.3 %copy.6 = f32[512,1024]{1,0:T(8,128)} copy(f32[512,1024]{1,0:T(8,128)S(1)} %get-tuple-element.4) | data formatting | bytes 4194304
  114.9 0.6 copy.7
Async XLA Ops:
  0.6 1.6 %copy-start = (f32[512,1024]{1,0:T(8,128)S(1)}, f32[512,1024]{1,0:T(8,128)}, u32[]{:S(2)}) copy-start(f32[512,1024]{1,0:T(8,128)} %x_hbm.1) | copy-start | bytes 6291460
  2.2 0.9 copy-start.1

commit v4 on v3

--- a/solution.py
+++ b/solution.py
@@ -19,7 +19,7 @@
 GROUP = 256
 PART = 128
 HALF = 512
-SHARES = ((0, 144), (144, 112), (256, 112), (368, 144))
+SHARES = ((0, 128), (128, 128), (256, 128), (384, 128))
 
 
 def split(value):
@@ -75,12 +75,11 @@
     for device in partners:
         pl.semaphore_signal(barrier, inc=1, device_id=device, device_id_type=MESH)
     own = pl.ds(pl.multiple_of(c * SHARE, SHARE), SHARE)
-    for u in range(4):
-        for i in range(2):
-            first_column = i * B + u * PART
-            rg[0, pl.ds(chip, 1), own, u * GROUP + i * PART : u * GROUP + (i + 1) * PART] = rot_ref[
-                0, :, :, first_column : first_column + PART
-            ]
+    for p in range(8):
+        i = jnp.where(pair == 3, p // 4, jnp.where(pair == 4, 1 - p // 4, p % 2))
+        h = jnp.where((pair == 3) | (pair == 4), p % 4, p // 2)
+        columns = pl.ds(pl.multiple_of(i * B + h * PART, PART), PART)
+        rg[0, pl.ds(chip, 1), own, p * PART : (p + 1) * PART] = rot_ref[0, :, :, columns]
     rg[1, pl.ds(chip, 1), own, :] = rot_ref[1]
     pl.semaphore_wait(barrier, len(partners))
 
@@ -139,15 +138,10 @@
         tile = dot3(high[:, :B], low[:, :B], high[:, B + o : B + o + n], low[:, B + o : B + o + n], ((0,), (0,)))
         cx[k, :, :, :, o : o + n] = tile.reshape(YS, ZS, CS * 8, n)
 
-    def norms(k, top, bottom):
-        for i, ref in enumerate((top, bottom)):
-            def add(step, total):
-                part = ref[pl.ds(pl.multiple_of(step * 32, 32), 32), :]
-                return total + jnp.sum((part * part).reshape(4, 8, B), axis=0)
-            total = lax.fori_loop(0, ROWS // 32, add, jnp.zeros((8, B), F32))
-            norm = jnp.sum(total, axis=0, keepdims=True)
-            for j in range(4):
-                nrm[k, 4 * i + j : 4 * i + j + 1, :] = norm[:, 128 * j : 128 * (j + 1)]
+    def norms():
+        for i in range(8):
+            block = x_ref[:, i * PART : (i + 1) * PART]
+            nrm[0, i : i + 1, :] = jnp.sum(block * block, axis=0, keepdims=True)
 
     mine = pl.ds(pl.multiple_of(c * 8, 8), 8)
     theirs = pl.ds(pl.multiple_of((1 - c) * 8, 8), 8)
@@ -225,120 +219,110 @@
         w_high, w_low = split(w)
         return dot3(high[...], low[...], w_high, w_low, ((1,), (0,)))
 
-    tops_up = (pair > 0) & (pair < PAIRS - 1) & (pair != 3)
-    bottoms_down = (pair > 0) & (pair != 4)
-
-    def up(g, i):
+    plain = (pair != 3) & (pair != 4)
+    tops_up = plain & (pair > 0) & (pair < PAIRS - 1)
+    bottoms_down = plain & (pair > 0)
+
+    def up(p, h):
         return pltpu.make_async_remote_copy(
-            src_ref=staged.at[g, :, pl.ds(i * PART, PART)], dst_ref=new.at[0, :, pl.ds(g * PART, PART)],
-            send_sem=ms.at[g, i], recv_sem=mr.at[g, 0], device_id=after, device_id_type=MESH,
+            src_ref=staged.at[p], dst_ref=new.at[0, :, pl.ds(h * PART, PART)],
+            send_sem=ms.at[p], recv_sem=mr.at[h, 0], device_id=after, device_id_type=MESH,
         )
 
-    def down(g):
+    def down(p, h):
         return pltpu.make_async_remote_copy(
-            src_ref=staged.at[g, :, pl.ds(PART, PART)], dst_ref=new.at[1, :, pl.ds(g * PART, PART)],
-            send_sem=ms.at[g, 1], recv_sem=mr.at[g, 1], device_id=before, device_id_type=MESH,
+            src_ref=staged.at[p], dst_ref=new.at[1, :, pl.ds(h * PART, PART)],
+            send_sem=ms.at[p], recv_sem=mr.at[h, 1], device_id=before, device_id_type=MESH,
         )
 
-    def far(g, i, j):
+    def far(p, i, j):
         rows = pl.ds(*SHARES[j])
         return pltpu.make_async_remote_copy(
-            src_ref=staged.at[g, rows, pl.ds(i * PART, PART)],
-            dst_ref=new.at[i, rows, pl.ds(g * PART, PART)] if j == 0 else passing.at[g, pl.ds(0, SHARES[j][1])],
-            send_sem=cs.at[g, j], recv_sem=cr.at[g, 0] if j == 0 else pr.at[g],
+            src_ref=staged.at[p, rows],
+            dst_ref=new.at[i, rows, pl.ds(p * PART, PART)] if j == 0 else passing.at[p, pl.ds(0, SHARES[j][1])],
+            send_sem=cs.at[p, j], recv_sem=cr.at[p, 0] if j == 0 else pr.at[p],
             device_id=(row, 4 - i if j == 0 else (3 - j, 4 + j)[i]), device_id_type=MESH,
         )
 
-    def passed(g, i, j):
+    def passed(p, i, j):
         return pltpu.make_async_remote_copy(
-            src_ref=passing.at[g, pl.ds(0, SHARES[j][1])], dst_ref=new.at[i, pl.ds(*SHARES[j]), pl.ds(g * PART, PART)],
-            send_sem=ps.at[g], recv_sem=cr.at[g, j], device_id=(row, 4 - i), device_id_type=MESH,
+            src_ref=passing.at[p, pl.ds(0, SHARES[j][1])], dst_ref=new.at[i, pl.ds(*SHARES[j]), pl.ds(p * PART, PART)],
+            send_sem=ps.at[p], recv_sem=cr.at[p, j], device_id=(row, 4 - i), device_id_type=MESH,
         )
 
-    def move(g, i):
-        @pl.when(pair == 3 + i)
-        def _():
-            for j in (1, 2, 3, 0):
-                far(g, i, j).start()
-
+    def sends(p):
+        i, h = p % 2, p // 2
+        if p < 4:
+            found = [(pair == 3 + k, [far(p, k, j) for j in (1, 2, 3, 0)]) for k in range(2)]
+        else:
+            found = [(pair == 3, [down(p, p - 4)]), (pair == 4, [up(p, p - 4)])]
         if i == 0:
-            @pl.when(tops_up)
+            return found + [(tops_up, [up(p, h)])]
+        return found + [(pair == 0, [up(p, h)]), (bottoms_down, [down(p, h)])]
+
+    def move(p):
+        for who, copies in sends(p):
+            @pl.when(who)
             def _():
-                up(g, 0).start()
-        else:
-            @pl.when(pair == 0)
+                for copy in copies:
+                    copy.start()
+
+        if p % 2 == 0:
+            for k, at_pair in enumerate((0, PAIRS - 1)):
+                @pl.when(pair == at_pair)
+                def _():
+                    new[k, :, p // 2 * PART : (p // 2 + 1) * PART] = staged[p]
+
+    def sent(p):
+        for who, copies in sends(p):
+            @pl.when(who)
             def _():
-                up(g, 1).start()
-
-            @pl.when(bottoms_down)
-            def _():
-                down(g).start()
-
-        if i == 0:
-            for p in (0, PAIRS - 1):
-                @pl.when(pair == p)
-                def _():
-                    new[p // (PAIRS - 1), :, g * PART : (g + 1) * PART] = staged[g, :, :PART]
-
-    def pass_on(g):
+                for copy in copies:
+                    copy.wait_send()
+
+        if p < 4:
+            for i in range(2):
+                for j in range(1, 4):
+                    @pl.when(pair == (3 - j, 4 + j)[i])
+                    def _():
+                        passed(p, i, j).wait_send()
+
+    def pass_on(p):
         for i in range(2):
             for j in range(1, 4):
                 @pl.when(pair == (3 - j, 4 + j)[i])
                 def _():
-                    far(g, i, j).wait_recv()
-                    passed(g, i, j).start()
-
-    def arrived(g):
+                    far(p, i, j).wait_recv()
+                    passed(p, i, j).start()
+
+    def arrived(h):
         @pl.when((pair > 0) & (pair != 4))
         def _():
-            up(g, 0).wait_recv()
+            up(0, h).wait_recv()
 
         @pl.when((pair < PAIRS - 1) & (pair != 3))
         def _():
-            down(g).wait_recv()
+            down(0, h).wait_recv()
 
         for i in range(2):
             @pl.when(pair == 4 - i)
             def _():
-                far(g, i, 0).wait_recv()
+                far(h, i, 0).wait_recv()
                 for j in range(1, 4):
-                    passed(g, i, j).wait_recv()
-
-            cols = slice(g * PART, (g + 1) * PART)
-            into = slice(i * B + g * PART, i * B + (g + 1) * PART)
-            nh[:, into], nl[:, into] = split(new[i, :, cols])
-
-    def sent(g):
-        for i in range(2):
-            @pl.when(pair == 3 + i)
-            def _():
-                for j in range(4):
-                    far(g, i, j).wait_send()
-
-            for j in range(1, 4):
-                @pl.when(pair == (3 - j, 4 + j)[i])
-                def _():
-                    passed(g, i, j).wait_send()
-
-        @pl.when(tops_up)
-        def _():
-            up(g, 0).wait_send()
-
-        @pl.when(pair == 0)
-        def _():
-            up(g, 1).wait_send()
-
-        @pl.when(bottoms_down)
-        def _():
-            down(g).wait_send()
+                    passed(h, i, j).wait_recv()
+
+            into = slice(i * B + h * PART, i * B + (h + 1) * PART)
+            block = new[i, :, h * PART : (h + 1) * PART]
+            nh[:, into], nl[:, into] = split(block)
+            nrm[1, 4 * i + h : 4 * i + h + 1, :] = jnp.sum(block * block, axis=0, keepdims=True)
 
     def first(u):
         gather_done(u)
         _, o, n = units[u]
-        g, start = o // GROUP, o % GROUP
-        staged[g, :, start : start + n] = turn(0, xh, xl, o, n)
-        for i in range(start // PART, (start + n) // PART):
-            move(g, i)
+        value = turn(0, xh, xl, o, n)
+        for k in range(n // PART):
+            staged[o // PART + k] = value[:, k * PART : (k + 1) * PART]
+            move(o // PART + k)
 
     def second(g):
         out_ref[:, g * GROUP : (g + 1) * GROUP] = turn(1, nh, nl, g * GROUP, GROUP)
@@ -348,7 +332,7 @@
     gather_z1(2)
     x_copy.wait()
     xh[...], xl[...] = split(x_ref[...])
-    norms(0, x_ref.at[:, :B], x_ref.at[:, B:])
+    norms()
     gram(0, xh, xl, 0, B)
     reduce_c(0)
     gather_z2(0)
@@ -361,10 +345,10 @@
     gather_z2(3)
     gather_y1(2)
     gather_z2(4)
+    gather_z1(5)
+    gather_z1(6)
     gather_c(0)
     gather_c(1)
-    gather_z1(5)
-    gather_z1(6)
     gather_y2(2)
     gather_y1(3)
     first(0)
@@ -372,42 +356,41 @@
     gather_y1(4)
     gather_c(2)
     gather_y2(3)
+    pass_on(0)
+    pass_on(1)
     gather_z2(5)
-    pass_on(0)
     first(2)
     gather_y2(4)
     reduce_y(0)
     gather_c(3)
     gather_z2(6)
     first(3)
-    pass_on(1)
+    pass_on(2)
+    pass_on(3)
     gather_c(4)
     first(4)
     gather_y1(5)
-    pass_on(2)
-    pass_on(3)
     gather_y1(6)
-    gather_y2(5)
-    gather_y2(6)
     arrived(0)
     arrived(1)
     arrived(2)
     arrived(3)
-    norms(1, new.at[0], new.at[1])
     gram(1, nh, nl, 0, GROUP)
     reduce_c(1)
     gram(1, nh, nl, GROUP, GROUP)
     reduce_c(2)
-    gather_c(5)
-    reduce_z(0)
     reduce_y(1)
     reduce_y(2)
+    gather_y2(5)
+    gather_y2(6)
+    reduce_z(0)
+    reduce_z(1)
+    reduce_z(2)
+    gather_c(5)
     gather_c(6)
     gather_done(5)
     second(0)
     second(1)
-    reduce_z(1)
-    reduce_z(2)
     gather_done(6)
     second(2)
     second(3)
@@ -415,8 +398,8 @@
     couple(1)
     for copy in pending:
         copy.wait_send()
-    for g in range(4):
-        sent(g)
+    for p in range(8):
+        sent(p)
 
 
 def per_device(matrix, rotations):
@@ -426,7 +409,7 @@
         pltpu.VMEM((ROWS, W), BF16),
         pltpu.VMEM((ROWS, W), BF16),
         pltpu.VMEM((2, YS * ZS, CS * SHARE, W), F32),
-        pltpu.VMEM((4, ROWS, GROUP), F32),
+        pltpu.VMEM((8, ROWS, PART), F32),
         pltpu.VMEM((2, ROWS, B), F32),
         pltpu.VMEM((ROWS, W), BF16),
         pltpu.VMEM((ROWS, W), BF16),
@@ -444,7 +427,7 @@
         pltpu.SemaphoreType.DMA,
         pltpu.SemaphoreType.DMA((7, 12)),
         pltpu.SemaphoreType.DMA((7, 12)),
-        pltpu.SemaphoreType.DMA((4, 2)),
+        pltpu.SemaphoreType.DMA((8,)),
         pltpu.SemaphoreType.DMA((4, 2)),
         pltpu.SemaphoreType.DMA((3, 15)),
         pltpu.SemaphoreType.DMA((3, 15)),

time: 116 us -> 111 us (0.957); the launches traced: 115 us -> 109 us
  Pallas kernels: 110 us -> 104 us
    pallas_call x1, Pallas kernels: 110 us -> 104 us  [per_device(): pl.pallas_call(body, name='tournament', out_shape=(jax.ShapeDtypeStruct((...]
where the time goes in v4:
time: 111 us; the launch traced here: 109 us
  Pallas kernels  104 us (94%)
  local copies, waits for them, and re-layouts  4.42 us (4%)
    pallas_call x1, Pallas kernels, per_device(): pl.pallas_call(body, name='tournament', out_shape=(jax.ShapeDtypeStruct((...  104 us
    unnamed x6, local copies, waits for them, and re-layouts  4.42 us

profile of v4, /device:TPU:1, one launch (start us, length us, event | category | flops | bytes accessed | tf_op | source)
XLA Modules:
  0.0 109.1 jit_solution(1027523118253927820)
XLA Ops:
  0.6 0.0 copy-start
  0.6 1.6 %copy-done = f32[512,1024]{1,0:T(8,128)S(1)} copy-done((f32[512,1024]{1,0:T(8,128)S(1)}, f32[512,1024]{1,0:T(8,128)}, u32[]{:S(2)}) %copy-start) | copy-done | bytes 2097176
  2.2 0.0 copy-start.1
  2.2 0.9 copy-done.1
  3.1 104.0 %tournament.1 = (f32[512,1024]{1,0:T(8,128)S(1)}, f32[2,1,8,512]{3,2,1,0:T(8,128)S(1)}) custom-call(f32[512,1024]{1,0:T(8,128)S(1)} %copy-done, f32[2,1,16,1024]{3,2,1,0:T(8,128)S(1)} %copy-done.1), custom_call_target="tpu_custom_call" | custom-call | tf_op jit(solution)/shard_map/tournament/pallas_call | solution.py:439
  107.1 1.3 %copy.6 = f32[512,1024]{1,0:T(8,128)} copy(f32[512,1024]{1,0:T(8,128)S(1)} %get-tuple-element.4) | data formatting | bytes 4194304
  108.4 0.6 copy.7
Async XLA Ops:
  0.6 1.6 %copy-start = (f32[512,1024]{1,0:T(8,128)S(1)}, f32[512,1024]{1,0:T(8,128)}, u32[]{:S(2)}) copy-start(f32[512,1024]{1,0:T(8,128)} %x_hbm.1) | copy-start | bytes 6291460
  2.2 0.9 copy-start.1

commit v5 on v4

--- a/solution.py
+++ b/solution.py
@@ -370,9 +370,9 @@
     gather_c(4)
     first(4)
     gather_y1(5)
-    gather_y1(6)
     arrived(0)
     arrived(1)
+    gather_y1(6)
     arrived(2)
     arrived(3)
     gram(1, nh, nl, 0, GROUP)
@@ -391,10 +391,10 @@
     gather_done(5)
     second(0)
     second(1)
+    couple(0)
     gather_done(6)
     second(2)
     second(3)
-    couple(0)
     couple(1)
     for copy in pending:
         copy.wait_send()

time: 111 us -> 111 us (level)
  no operation moved by 1% of the time
where the time goes in v5:
time: 111 us; the launch traced here: 109 us
  Pallas kernels  104 us (94%)
  local copies, waits for them, and re-layouts  4.42 us (4%)
    pallas_call x1, Pallas kernels, per_device(): pl.pallas_call(body, name='tournament', out_shape=(jax.ShapeDtypeStruct((...  104 us
    unnamed x6, local copies, waits for them, and re-layouts  4.42 us

profile of v5, /device:TPU:1, one launch (start us, length us, event | category | flops | bytes accessed | tf_op | source)
XLA Modules:
  0.0 109.1 jit_solution(16714327611302351620)
XLA Ops:
  0.6 0.0 copy-start
  0.6 1.6 %copy-done = f32[512,1024]{1,0:T(8,128)S(1)} copy-done((f32[512,1024]{1,0:T(8,128)S(1)}, f32[512,1024]{1,0:T(8,128)}, u32[]{:S(2)}) %copy-start) | copy-done | bytes 2097176
  2.2 0.0 copy-start.1
  2.2 0.9 copy-done.1
  3.1 104.0 %tournament.1 = (f32[512,1024]{1,0:T(8,128)S(1)}, f32[2,1,8,512]{3,2,1,0:T(8,128)S(1)}) custom-call(f32[512,1024]{1,0:T(8,128)S(1)} %copy-done, f32[2,1,16,1024]{3,2,1,0:T(8,128)S(1)} %copy-done.1), custom_call_target="tpu_custom_call" | custom-call | tf_op jit(solution)/shard_map/tournament/pallas_call | solution.py:439
  107.1 1.3 %copy.6 = f32[512,1024]{1,0:T(8,128)} copy(f32[512,1024]{1,0:T(8,128)S(1)} %get-tuple-element.4) | data formatting | bytes 4194304
  108.4 0.6 copy.7
Async XLA Ops:
  0.6 1.6 %copy-start = (f32[512,1024]{1,0:T(8,128)S(1)}, f32[512,1024]{1,0:T(8,128)}, u32[]{:S(2)}) copy-start(f32[512,1024]{1,0:T(8,128)} %x_hbm.1) | copy-start | bytes 6291460
  2.2 0.9 copy-start.1
